TPU v7x, 32 devices: a whole 2x2x4 slice. The times are simulated.
32 devices in a mesh: fsdp: 32 (over z, y, x, core).
Axes of the slice: x: 2, y: 2, z: 4, core: 2. Of those that a mesh axis runs over, the one named last changes fastest.
Arguments:
- tokens: bfloat16 [12608, 768], P('fsdp'), may hold values from -6 to 6
- ln1_gain: bfloat16 [768], P('fsdp'), may hold values from 0.5 to 1.5
- ln1_shift: bfloat16 [768], P('fsdp'), may hold values from -3 to 3
- qkv_weight: bfloat16 [768, 2304], P('fsdp'), may hold values from -0.21875 to 0.21875
- qv_bias: bfloat16 [2, 768], P(None, 'fsdp'), may hold values from -3 to 3
- proj_weight: bfloat16 [768, 768], P('fsdp'), may hold values from -1 to 1
- proj_bias: bfloat16 [768], P('fsdp'), may hold values from -3 to 3
- ln2_gain: bfloat16 [768], P('fsdp'), may hold values from 0.5 to 1.5
- ln2_shift: bfloat16 [768], P('fsdp'), may hold values from -3 to 3
- router_weight: bfloat16 [768, 4], P('fsdp'), may hold values from -0.15625 to 0.15625
- expert_in: bfloat16 [3072, 4, 768], P('fsdp'), may hold values from -0.21875 to 0.21875
- expert_in_bias: bfloat16 [3072, 4], P('fsdp'), may hold values from -3 to 3
- expert_out: bfloat16 [3072, 4, 768], P('fsdp'), may hold values from -0.3125 to 0.3125
- expert_out_bias: bfloat16 [4, 768], P(None, 'fsdp'), may hold values from -3 to 3
- routes: int32 [12608, 2], P('fsdp'), may hold values from 0 to 3, all different within a row; in each aligned block of 394 rows (0 to 393, 394 to 787, ...) at most 246 rows name the same one
- out_grad: bfloat16 [12608, 768], P('fsdp'), may hold values from -6 to 6
Outputs:
- block_out: bfloat16 [12608, 768], P('fsdp')
- tokens_grad: float32 [12608, 768], P('fsdp')
- ln1_gain_grad: float32 [768], P('fsdp')
- ln1_shift_grad: float32 [768], P('fsdp')
- qkv_weight_grad: float32 [768, 2304], P('fsdp')
- qv_bias_grad: float32 [2, 768], P(None, 'fsdp')
- proj_weight_grad: float32 [768, 768], P('fsdp')
- proj_bias_grad: float32 [768], P('fsdp')
- ln2_gain_grad: float32 [768], P('fsdp')
- ln2_shift_grad: float32 [768], P('fsdp')
- router_weight_grad: float32 [768, 4], P('fsdp')
- expert_in_grad: float32 [3072, 4, 768], P('fsdp')
- expert_in_bias_grad: float32 [3072, 4], P('fsdp')
- expert_out_grad: float32 [3072, 4, 768], P('fsdp')
- expert_out_bias_grad: float32 [4, 768], P(None, 'fsdp')
Inputs may be any that keep to these rules, and one draw needn't show every extreme that they name: `routes`: each row names 2 different experts. Within the rows of one device no expert is named more than 246 times, and in some blocks one expert is named exactly 246 times.
All inputs are finite; a program needn't handle non-finite values.
Results may differ from a plain program's by a relative error of at most 0.015.
Values may be sent and summed in bfloat16 or wider, within the bound.
A program may use at most 320 MiB of HBM per device.

v0:
```python
import functools
import jax
import jax.numpy as jnp
from jax import lax
from jax.sharding import PartitionSpec as P

HEADS = 12
HD = 64
EXPERTS = 4
TOP = 2
LEN = 197
SEQ_DEV = 2
SLOTS = 256
SMALL_ROWS = 8


def layer_norm(values, gain_vec, shift_vec):
    row_mean = jnp.mean(values, axis=-1, keepdims=True)
    centred = values - row_mean
    spread = jnp.mean(centred * centred, axis=-1, keepdims=True)
    return centred * lax.rsqrt(spread + 1e-06) * gain_vec + shift_vec


def gelu_tanh(values):
    return jax.nn.gelu(values, approximate=True)


def take_rows(block, widths):
    pieces, at = ([], 0)
    for width in widths:
        pieces.append(block[:, at : at + width])
        at += width
    return pieces


def dot_f32(left, right, left_dim, right_dim):
    return lax.dot_general(
        left, right, (((left_dim,), (right_dim,)), ((), ())), preferred_element_type=jnp.float32
    )


def on_device(
    n_dev,
    tokens,
    ln1_gain,
    ln1_shift,
    qkv_weight,
    qv_bias,
    proj_weight,
    proj_bias,
    ln2_gain,
    ln2_shift,
    router_weight,
    expert_in,
    expert_in_bias,
    expert_out,
    expert_out_bias,
    routes,
    out_grad,
):
    highest = lax.Precision.HIGHEST
    f32 = jnp.float32
    low = jnp.bfloat16
    row_count, model_width = tokens.shape
    shape_four = (SEQ_DEV, LEN, HEADS, HD)
    query_scale = HD ** (-0.5)
    own = qkv_weight.shape[0]
    units = expert_in.shape[0]
    wide = 4 * model_width
    core = lax.axis_index("fsdp") % 2
    same_core = [list(range(c, n_dev, 2)) for c in range(2)]
    swap = [(i, i ^ 1) for i in range(n_dev)]
    small_parts = [
        ln1_gain,
        ln1_shift,
        qv_bias.reshape(-1),
        proj_bias,
        ln2_gain,
        ln2_shift,
        router_weight.T.reshape(-1),
        expert_out_bias.reshape(-1),
        expert_in_bias.T.reshape(-1),
    ]
    small_widths = [p.shape[0] for p in small_parts]
    small_total = sum(small_widths)
    small_mine = jnp.pad(
        jnp.concatenate(small_parts)[None, :], ((0, SMALL_ROWS - 1), (0, wide - small_total))
    )
    dense_mine = jnp.concatenate(
        [jnp.concatenate([qkv_weight, proj_weight], axis=1), small_mine], axis=0
    )
    dense = lax.all_gather(dense_mine, "fsdp", axis=0, tiled=True)
    dense = dense.reshape(n_dev, own + SMALL_ROWS, wide)
    w_in = lax.all_gather(
        expert_in.reshape(units, EXPERTS * model_width),
        "fsdp",
        axis=0,
        tiled=True,
        axis_index_groups=same_core,
    )
    w_out = lax.all_gather(
        expert_out.reshape(units, EXPERTS * model_width),
        "fsdp",
        axis=0,
        tiled=True,
        axis_index_groups=same_core,
    )
    weights = dense[:, :own, :].reshape(n_dev * own, wide)
    w_qkv = weights[:, : 3 * model_width]
    w_proj = weights[:, 3 * model_width :]
    gain1, shift1, bias_qv, bias_proj, gain2, shift2, w_router, bias_out, bias_in = take_rows(
        dense[:, own, :], small_widths
    )
    gain1 = gain1.reshape(-1).astype(f32)
    shift1 = shift1.reshape(-1).astype(f32)
    gain2 = gain2.reshape(-1).astype(f32)
    shift2 = shift2.reshape(-1).astype(f32)
    bias_proj = bias_proj.reshape(-1).astype(f32)
    bias_q = bias_qv[:, :own].reshape(-1).astype(f32)
    bias_v = bias_qv[:, own:].reshape(-1).astype(f32)
    w_router = jnp.stack([p.reshape(-1) for p in take_rows(w_router, [own] * EXPERTS)])
    bias_out = [p.reshape(-1).astype(f32) for p in take_rows(bias_out, [own] * EXPERTS)]
    bias_in = lax.dynamic_index_in_dim(
        bias_in.reshape(n_dev // 2, 2, EXPERTS * units), core, axis=1, keepdims=False
    )
    bias_in = [p.reshape(-1).astype(f32) for p in take_rows(bias_in, [units] * EXPERTS)]
    experts = jnp.arange(EXPERTS, dtype=jnp.int32)[None, :]
    pick = [(routes[:, j : j + 1] == experts).astype(f32) for j in range(TOP)]
    picked = pick[0] + pick[1]
    tri = jnp.arange(row_count)[:, None] > jnp.arange(row_count)[None, :]
    before = dot_f32(tri.astype(low), picked.astype(low), 1, 0)
    slot_ids = jnp.arange(EXPERTS * SLOTS, dtype=jnp.int32)[None, :]
    hit = []
    for j in range(TOP):
        slot = jnp.sum(pick[j] * before, axis=1, keepdims=True).astype(jnp.int32)
        hit.append(slot_ids == routes[:, j : j + 1] * SLOTS + slot)
    dispatch = (hit[0] | hit[1]).astype(low)
    inputs = tokens.astype(f32)
    normed_full, norm1_pull = jax.vjp(layer_norm, inputs, gain1, shift1)
    normed = normed_full.astype(low)
    projected = jnp.dot(normed, w_qkv, preferred_element_type=f32)
    queries = ((projected[:, :model_width] + bias_q) * query_scale).astype(low).reshape(shape_four)
    key_rows = projected[:, model_width : 2 * model_width].astype(low).reshape(shape_four)
    values = (projected[:, 2 * model_width :] + bias_v).astype(low).reshape(shape_four)
    scores = jnp.einsum("sqhd,skhd->shqk", queries, key_rows, preferred_element_type=f32)
    exp_scores = jnp.exp(scores - jnp.max(scores, axis=-1, keepdims=True))
    probs_full = exp_scores / jnp.sum(exp_scores, axis=-1, keepdims=True)
    probs_low = probs_full.astype(low)
    attended = jnp.einsum("shqk,skhd->sqhd", probs_low, values, preferred_element_type=f32)
    attended = attended.reshape(row_count, model_width).astype(low)
    middle = inputs + jnp.dot(attended, w_proj, preferred_element_type=f32) + bias_proj
    normed2_full, norm2_pull = jax.vjp(layer_norm, middle, gain2, shift2)
    normed2 = normed2_full.astype(low)
    gate_probs = jax.nn.softmax(dot_f32(normed2, w_router, 1, 1), axis=-1)
    chosen = [jnp.sum(gate_probs * pick[j], axis=1, keepdims=True) for j in range(TOP)]
    combine = (jnp.where(hit[0], chosen[0], 0.0) + jnp.where(hit[1], chosen[1], 0.0)).astype(low)

    def pair_rows(mine):
        mine = mine.reshape(EXPERTS, SLOTS, model_width)
        theirs = lax.ppermute(mine, "fsdp", swap)
        return [jnp.concatenate([mine[e], theirs[e]], axis=0) for e in range(EXPERTS)]

    def pair_sum(partial):
        sent = jnp.stack([p[SLOTS:].astype(low) for p in partial])
        got = lax.ppermute(sent, "fsdp", swap)
        return [p[:SLOTS] + got[e].astype(f32) for e, p in enumerate(partial)]

    slot_rows = pair_rows(dot_f32(dispatch, normed2, 0, 0).astype(low))
    grad_result_mine = dot_f32(combine, out_grad, 0, 0).astype(low)
    grad_result = pair_rows(grad_result_mine)

    def expert(weight, e):
        return weight[:, e * model_width : (e + 1) * model_width]

    def scatter_units(terms):
        return lax.psum_scatter(
            terms, "fsdp", scatter_dimension=0, tiled=True, axis_index_groups=same_core
        )

    each = range(EXPERTS)
    pre_act = [dot_f32(slot_rows[e], expert(w_in, e), 1, 1) + bias_in[e] for e in each]
    hidden, pulls = ([], [])
    for e in each:
        out, pull = jax.vjp(gelu_tanh, pre_act[e])
        hidden.append(out.astype(low))
        pulls.append(pull)
    out_terms = [dot_f32(hidden[e], grad_result[e], 0, 0).astype(low) for e in each]
    out_terms = jnp.concatenate(out_terms, axis=1)
    grad_pre = [
        pulls[e](dot_f32(grad_result[e], expert(w_out, e), 1, 1))[0].astype(low) for e in each
    ]
    in_terms = [dot_f32(grad_pre[e], slot_rows[e], 0, 0).astype(low) for e in each]
    in_terms = jnp.concatenate(in_terms, axis=1)
    out_terms, in_terms, hidden, grad_pre = lax.optimization_barrier(
        (out_terms, in_terms, hidden, grad_pre)
    )
    expert_out_mine = scatter_units(out_terms)
    expert_in_mine = scatter_units(in_terms)
    grad_bias_in = jnp.stack([jnp.sum(grad_pre[e].astype(f32), axis=0) for e in each])
    summed = pair_sum([dot_f32(hidden[e], expert(w_out, e), 1, 0) for e in each])
    result = jnp.concatenate([(summed[e] + bias_out[e]).astype(low) for e in each], axis=0)
    grad_slots = pair_sum([dot_f32(grad_pre[e], expert(w_in, e), 1, 0) for e in each])
    grad_slots = jnp.concatenate([g.astype(low) for g in grad_slots], axis=0)
    block_out = (middle + jnp.dot(combine, result, preferred_element_type=f32)).astype(low)
    grad_top = out_grad.astype(f32)
    slot_dots = dot_f32(out_grad, result, 1, 1) * dispatch.astype(f32)
    grad_gates = jnp.concatenate(
        [jnp.sum(slot_dots[:, e * SLOTS : (e + 1) * SLOTS], axis=1, keepdims=True) for e in each],
        axis=1,
    )
    grad_logits = gate_probs * (
        grad_gates - jnp.sum(gate_probs * grad_gates, axis=-1, keepdims=True)
    )
    grad_router = jnp.dot(grad_logits.T, normed2.astype(f32), precision=highest)
    grad_normed2 = jnp.dot(grad_logits, w_router.astype(f32), precision=highest)
    grad_normed2 = grad_normed2 + jnp.dot(dispatch, grad_slots, preferred_element_type=f32)
    grad_mid_norm, grad_gain2, grad_shift2 = norm2_pull(grad_normed2)
    grad_middle = grad_top + grad_mid_norm
    grad_branch = grad_middle.astype(low)
    grad_bias_proj = jnp.sum(grad_branch.astype(f32), axis=0)
    grad_proj = dot_f32(attended, grad_branch, 0, 0)
    grad_attended = dot_f32(grad_branch, w_proj, 1, 1).astype(low).reshape(shape_four)
    grad_probs = jnp.einsum("sqhd,skhd->shqk", grad_attended, values, preferred_element_type=f32)
    grad_values = jnp.einsum(
        "shqk,sqhd->skhd", probs_low, grad_attended, preferred_element_type=f32
    ).astype(low)
    grad_scores = (
        probs_full * (grad_probs - jnp.sum(probs_full * grad_probs, axis=-1, keepdims=True))
    ).astype(low)
    grad_queries = jnp.einsum(
        "shqk,skhd->sqhd", grad_scores, key_rows, preferred_element_type=f32
    ).astype(low)
    grad_keys = jnp.einsum(
        "shqk,sqhd->skhd", grad_scores, queries, preferred_element_type=f32
    ).astype(low)
    grad_query_pre = grad_queries.astype(f32).reshape(row_count, model_width) * query_scale
    grad_values = grad_values.reshape(row_count, model_width)
    grad_projected = jnp.concatenate(
        [grad_query_pre.astype(low), grad_keys.reshape(row_count, model_width), grad_values], axis=1
    )
    grad_qkv = dot_f32(normed, grad_projected, 0, 0)
    grad_normed = dot_f32(grad_projected, w_qkv, 1, 1)
    grad_in_norm, grad_gain1, grad_shift1 = norm1_pull(grad_normed)
    tokens_grad = grad_middle + grad_in_norm

    def by_owner(rows):
        return (
            rows.reshape(-1, n_dev, rows.shape[-1] // n_dev).transpose(1, 0, 2).reshape(n_dev, -1)
        )

    here = (jnp.arange(2) == core).astype(f32)
    bias_in_slots = grad_bias_in.reshape(EXPERTS, n_dev // 2, 1, units) * here[None, None, :, None]
    grad_bias_out = jnp.sum(
        grad_result_mine.astype(f32).reshape(EXPERTS, SLOTS, model_width), axis=1
    )
    small_grads = jnp.concatenate(
        [
            by_owner(
                jnp.concatenate(
                    [
                        jnp.stack(
                            [
                                grad_gain1,
                                grad_shift1,
                                jnp.sum(grad_query_pre, axis=0),
                                jnp.sum(grad_values.astype(f32), axis=0),
                                grad_bias_proj,
                                grad_gain2,
                                grad_shift2,
                            ]
                        ),
                        grad_router,
                        grad_bias_out,
                    ],
                    axis=0,
                )
            ),
            by_owner(bias_in_slots.reshape(EXPERTS, n_dev * units)),
        ],
        axis=1,
    ).astype(low)
    small_grads = jnp.pad(
        small_grads[:, None, :], ((0, 0), (0, SMALL_ROWS - 1), (0, wide - small_total))
    )
    dense_grads = jnp.concatenate([grad_qkv.astype(low), grad_proj.astype(low)], axis=1)
    dense_grads = jnp.concatenate([dense_grads.reshape(n_dev, own, wide), small_grads], axis=1)
    dense_grads, expert_out_mine, expert_in_mine = lax.optimization_barrier(
        (dense_grads, expert_out_mine, expert_in_mine)
    )
    dense_out = lax.psum_scatter(
        dense_grads.reshape(n_dev * (own + SMALL_ROWS), wide),
        "fsdp",
        scatter_dimension=0,
        tiled=True,
    ).astype(f32)
    small = [p[0] for p in take_rows(dense_out[own : own + 1], small_widths)]
    expert_shape = (units, EXPERTS, model_width)
    return (
        block_out,
        tokens_grad,
        small[0],
        small[1],
        dense_out[:own, : 3 * model_width],
        small[2].reshape(2, own),
        dense_out[:own, 3 * model_width :],
        small[3],
        small[4],
        small[5],
        small[6].reshape(EXPERTS, own).T,
        expert_in_mine.astype(f32).reshape(expert_shape),
        small[8].reshape(EXPERTS, units).T,
        expert_out_mine.astype(f32).reshape(expert_shape),
        small[7].reshape(EXPERTS, own),
    )


def solution(mesh):
    in_specs = (
        P("fsdp", None),
        P("fsdp"),
        P("fsdp"),
        P("fsdp", None),
        P(None, "fsdp"),
        P("fsdp", None),
        P("fsdp"),
        P("fsdp"),
        P("fsdp"),
        P("fsdp", None),
        P("fsdp", None, None),
        P("fsdp", None),
        P("fsdp", None, None),
        P(None, "fsdp"),
        P("fsdp", None),
        P("fsdp", None),
    )
    out_specs = (
        P("fsdp", None),
        P("fsdp", None),
        P("fsdp"),
        P("fsdp"),
        P("fsdp", None),
        P(None, "fsdp"),
        P("fsdp", None),
        P("fsdp"),
        P("fsdp"),
        P("fsdp"),
        P("fsdp", None),
        P("fsdp", None, None),
        P("fsdp", None),
        P("fsdp", None, None),
        P(None, "fsdp"),
    )
    return jax.shard_map(
        functools.partial(on_device, mesh.shape["fsdp"]),
        mesh=mesh,
        in_specs=in_specs,
        out_specs=out_specs,
        check_vma=False,
    )
```

profile of v0, /device:TPU:0, one launch (start us, length us, event | category | flops | bytes accessed | tf_op | source)
XLA Modules:
  0.0 876.5 jit_solution(18161666276513297244)
XLA Ops:
  10.4 3.4 concatenate.97
  19.7 68.1 %all-gather.4.cloned.1.call-done = bf16[1024,3072]{1,0:T(8,128)(2,1)} async-done(((bf16[32,3072]{1,0:T(8,128)(2,1)}), bf16[1024,3072]{1,0:T(8,128)(2,1)}) %all-gather.4.cloned.1.call-update) | async-done | bytes 6291472 | tf_op jit(solution)/shard_map/all_gather | solution.py:92
  89.4 4.8 slice.421
  99.1 3.8 fusion.33
  107.0 3.4 reshape.485
  114.7 2.4 copy.104
  117.1 3.8 fusion.179
  120.9 3.0 fusion.90
  130.1 2.6 bitcast_reduce_fusion
  133.0 2.4 convolution_convert_fusion.10
  136.9 2.4 fusion.177
  139.4 2.4 fusion.176
  141.8 2.6 slice_bitcast_fusion.14
  144.4 2.5 slice_bitcast_fusion.15
  146.9 65.3 %all-gather.6.cloned.1.call-done = bf16[1536,3072]{1,0:T(8,128)(2,1)} async-done(((bf16[96,3072]{1,0:T(8,128)(2,1)}), bf16[1536,3072]{1,0:T(8,128)(2,1)}) %all-gather.6.cloned.1.call-update) | async-done | bytes 9437200 | tf_op jit(solution)/shard_map/all_gather | solution.py:94
  212.2 5.7 multiply_convert_fusion.4
  219.0 2.9 convolution_convert_fusion.8
  221.9 113.8 %all-gather.8.cloned.1.call-done = bf16[1536,3072]{1,0:T(8,128)(2,1)} async-done(((bf16[96,3072]{1,0:T(8,128)(2,1)}), bf16[1536,3072]{1,0:T(8,128)(2,1)}) %all-gather.8.cloned.1.call-update) | async-done | bytes 9437200 | tf_op jit(solution)/shard_map/all_gather | solution.py:101
  335.6 6.2 fusion.9
  343.6 3.7 multiply_convert_fusion.1
  348.9 4.9 fusion.30
  359.3 4.6 fusion.23
  369.0 4.6 fusion.16
  375.9 4.4 pad_maximum_fusion
  380.2 4.3 pad_maximum_fusion.1
  384.5 12.6 %copy.130 = bf16[1536,3072]{1,0:T(8,128)(2,1)} copy(bf16[1536,3072]{0,1:T(8,128)(2,1)} %pad_maximum_fusion) | data formatting | bytes 18874368
  397.2 12.7 %copy.132 = bf16[1536,3072]{1,0:T(8,128)(2,1)} copy(bf16[1536,3072]{0,1:T(8,128)(2,1)} %pad_maximum_fusion.1) | data formatting | bytes 18874368
  411.1 3.7 fusion.53
  414.8 4.2 fusion.47
  426.3 2.6 fusion.68
  428.9 2.6 fusion.62
  431.5 2.5 fusion.59
  436.2 3.6 fusion.65
  444.0 2.9 fusion.125
  449.1 2.7 fusion.117
  461.2 3.4 fusion.182
  466.8 3.4 multiply_reduce_fusion
  470.3 3.4 multiply_convert_fusion
  476.3 3.4 reshape.443
  486.2 5.1 fusion.171
  495.0 2.3 convolution_convert_fusion
  497.9 3.4 fusion.2
  501.3 65.2 %reduce-scatter.10.cloned.1.call-done = bf16[96,3072]{1,0:T(8,128)(2,1)} async-done(((bf16[1536,3072]{1,0:T(8,128)(2,1)}), bf16[96,3072]{1,0:T(8,128)(2,1)}) %reduce-scatter.10.cloned.1.call-update) | async-done | bytes 589840
  566.6 2.2 copy.131
  568.8 174.5 %reduce-scatter.12.cloned.1.call-done = bf16[96,3072]{1,0:T(8,128)(2,1)} async-done(((bf16[1536,3072]{1,0:T(8,128)(2,1)}), bf16[96,3072]{1,0:T(8,128)(2,1)}) %reduce-scatter.12.cloned.1.call-update) | async-done | bytes 589840
  743.3 2.2 copy.133
  746.9 2.8 add_add_fusion.2
  754.2 107.9 %reduce-scatter.8.cloned.1.call-done = bf16[32,3072]{1,0:T(8,128)(2,1)} async-done(((bf16[1024,3072]{1,0:T(8,128)(2,1)}), bf16[32,3072]{1,0:T(8,128)(2,1)}) %reduce-scatter.8.cloned.1.call-update) | async-done | bytes 196624 | tf_op jit(solution)/shard_map/reduce_scatter | solution.py:290
  (409 shorter events, 102.8 us)
Async XLA Ops:
  7.2 10.3 %copy-start.37 = (bf16[96,4,768]{2,1,0:T(4,128)(2,1)S(1)}, bf16[96,4,768]{2,1,0:T(4,128)(2,1)}, u32[]{:S(2)}) copy-start(bf16[96,4,768]{2,1,0:T(4,128)(2,1)} %param.28) | copy-start | bytes 1769476
  7.2 11.3 %copy-start.4 = (bf16[394,768]{1,0:T(8,128)(2,1)S(1)}, bf16[394,768]{1,0:T(8,128)(2,1)}, u32[]{:S(2)}) copy-start(bf16[394,768]{1,0:T(8,128)(2,1)} %param.16) | copy-start | bytes 1815556
  7.2 80.6 %all-gather.4.cloned.1.call-start = ((), (), s32[]{:S(2)}) async-start(), calls=%async_computation.3 | async-start | bytes 6488064 | tf_op jit(solution)/shard_map/all_gather | solution.py:92
  15.4 196.7 %all-gather.6.cloned.1.call-start = ((), (), s32[]{:S(2)}) async-start(), calls=%async_computation.4 | async-start | bytes 10027008 | tf_op jit(solution)/shard_map/all_gather | solution.py:94
  17.5 318.2 %all-gather.8.cloned.1.call-start = ((), (), s32[]{:S(2)}) async-start(), calls=%async_computation.5 | async-start | bytes 10027008 | tf_op jit(solution)/shard_map/all_gather | solution.py:101
  18.5 548.1 %reduce-scatter.10.cloned.1.call-start = ((), (), s32[]{:S(2)}) async-start(), calls=%async_computation.7 | async-start | bytes 10027008
  18.7 80.3 %copy-start.71 = (f32[394]{0:T(512)}, f32[394]{0:T(512)S(1)}, u32[]{:S(2)}) copy-start(f32[394]{0:T(512)S(1)} %broadcast_multiply_fusion.1) | copy-start | bytes 4732
  19.0 75.2 %copy-start.81 = (f32[394]{0:T(512)}, f32[394]{0:T(512)S(1)}, u32[]{:S(2)}) copy-start(f32[394]{0:T(512)S(1)} %fusion.96) | copy-start | bytes 4732
  19.1 80.0 %copy-start.85 = (f32[394]{0:T(512)}, f32[394]{0:T(512)S(1)}, u32[]{:S(2)}) copy-start(f32[394]{0:T(512)S(1)} %fusion.144) | copy-start | bytes 4732
  95.8 33.6 %copy-start.73 = (bf16[1,768]{1,0:T(2,128)(2,1)}, bf16[1,768]{1,0:T(2,128)(2,1)S(1)}, u32[]{:S(2)}) copy-start(bf16[1,768]{1,0:T(2,128)(2,1)S(1)} %stack_reshape.15) | copy-start | bytes 4612
  97.9 5.0 copy-start.67
  98.0 30.5 %copy-start.63 = (f32[768]{0:T(1024)}, f32[768]{0:T(1024)S(1)}, u32[]{:S(2)}) copy-start(f32[768]{0:T(1024)S(1)} %reshape.457) | copy-start | bytes 9220
  98.1 4.8 copy-start.90
  107.0 10.1 %copy-start.8 = (bf16[2,197,12,64]{1,3,2,0:T(8,128)(2,1)}, bf16[2,197,12,64]{1,3,2,0:T(8,128)(2,1)S(1)}, u32[]{:S(2)}) copy-start(bf16[2,197,12,64]{1,3,2,0:T(8,128)(2,1)S(1)} %copy.102) | copy-start | bytes 1815556
  107.0 5.6 copy-start.14
  112.5 8.3 copy-start.6
  117.1 3.8 copy-start.33
  128.1 326.3 %copy-start = (f32[394,768]{1,0:T(8,128)}, f32[394,768]{1,0:T(8,128)S(1)}, u32[]{:S(2)}) copy-start(f32[394,768]{1,0:T(8,128)S(1)} %get-tuple-element.184) | copy-start | bytes 3631108
  128.2 4.4 copy-start.65
  130.0 321.8 %copy-start.92 = (s32[394,1]{0,1:T(1,128)}, s32[394,1]{0,1:T(1,128)S(1)}, u32[]{:S(2)}) copy-start(s32[394,1]{0,1:T(1,128)S(1)} %get-tuple-element.177) | copy-start | bytes 4732
  130.0 321.8 %copy-start.94 = (s32[394,1]{0,1:T(1,128)}, s32[394,1]{0,1:T(1,128)S(1)}, u32[]{:S(2)}) copy-start(s32[394,1]{0,1:T(1,128)S(1)} %get-tuple-element.178) | copy-start | bytes 4732
  132.6 9.2 %collective-permute-start.1 = (bf16[4,256,768]{2,1,0:T(8,128)(2,1)}, bf16[4,256,768]{2,1,0:T(8,128)(2,1)}, u32[]{:S(2)}, u32[]{:S(2)}) collective-permute-start(bf16[4,256,768]{2,1,0:T(8,128)(2,1)} %bitcast.14), channel_id=1, source_target_pairs={{0,1},{1,0},{2,3},{3,2},{4,5},{5,4},{6,7},{7,6},{8,9},{9,8},{10,11... | collective-permute-start | bytes 4718600 | tf_op jit(solution)/shard_map/ppermute | solution.py:160
  135.4 8.9 %collective-permute-start = (bf16[4,256,768]{2,1,0:T(8,128)(2,1)}, bf16[4,256,768]{2,1,0:T(8,128)(2,1)}, u32[]{:S(2)}, u32[]{:S(2)}) collective-permute-start(bf16[4,256,768]{2,1,0:T(8,128)(2,1)} %bitcast.11), channel_id=1, source_target_pairs={{0,1},{1,0},{2,3},{3,2},{4,5},{5,4},{6,7},{7,6},{8,9},{9,8},{10,11... | collective-permute-start | bytes 4718600 | tf_op jit(solution)/shard_map/ppermute | solution.py:160
  212.2 6.8 copy-start.56
  212.2 6.8 copy-start.58
  335.6 6.3 copy-start.54
  335.6 6.3 copy-start.59
  347.4 7.9 slice-start
  348.8 6.5 slice-start.1
  348.9 6.5 slice-start.2
  397.2 346.1 %reduce-scatter.12.cloned.1.call-start = ((), (), s32[]{:S(2)}) async-start(), calls=%async_computation.8 | async-start | bytes 10027008
  409.9 452.1 %reduce-scatter.8.cloned.1.call-start = ((), (), s32[]{:S(2)}) async-start(), calls=%async_computation.6 | async-start | bytes 6488064 | tf_op jit(solution)/shard_map/reduce_scatter | solution.py:290
  411.1 8.1 slice-start.6
  411.1 8.1 slice-start.7
  414.8 4.3 copy-start.27
  414.8 4.4 slice-start.8
  414.8 4.4 copy-start.102
  419.2 5.0 slice-start.3
  419.2 6.2 slice-start.4
  421.2 4.6 slice-start.5
  424.2 4.7 copy-start.21
  424.2 19.7 %collective-permute-start.2 = (bf16[4,256,768]{2,1,0:T(8,128)(2,1)}, bf16[4,256,768]{2,1,0:T(8,128)(2,1)}, u32[]{:S(2)}, u32[]{:S(2)}) collective-permute-start(bf16[4,256,768]{2,1,0:T(8,128)(2,1)} %pad_maximum_fusion.3), channel_id=1, source_target_pairs={{0,1},{1,0},{2,3},{3,2},{4,5},{5,4},{6,7},{7,6},{8,9},{9,8},{10,11... | collective-permute-start | bytes 4718600 | tf_op jit(solution)/shard_map/ppermute | solution.py:165
  443.0 6.1 collective-permute-start.3
  474.6 5.1 copy-start.7
  481.3 4.6 copy-start.11
  486.1 5.2 copy-start.60
  486.1 5.2 copy-start.82
  486.2 5.2 copy-start.86
  (79 other events, 150.7 us)
Sparse Core Ops, SparseCore 0:
  15.5 72.1 all-gather.3
  91.2 120.9 all-gather.5
  215.0 120.6 all-gather.7
  397.3 169.2 reduce-scatter.9
  573.0 170.2 reduce-scatter.11
  748.8 113.1 reduce-scatter.7
where the time goes:
time: 884 us; the launch traced here: 877 us
  waiting for transfers between devices  595 us (67%)
  local copies, waits for them, and re-layouts  114 us (13%)
  matrix products  114 us (13%)
  other arithmetic  36 us (4%)
  between operations  16.4 us (2%)
    unnamed x8, waiting for transfers between devices  240 us
    all_gather x1, waiting for transfers between devices, on_device(): lax.all_gather(expert_out.reshape(units, EXPERTS * model_width), 'fsdp',...  114 us
    reduce_scatter x1, waiting for transfers between devices, on_device(): lax.psum_scatter(dense_grads.reshape(n_dev * (own + SMALL_ROWS), wide), '...  108 us
    dot_general x33, matrix products, dot_f32(): lax.dot_general(left, right, (((left_dim,), (right_dim,)), ((), ())), pre...  87.3 us
    all_gather x1, waiting for transfers between devices, on_device(): dense = lax.all_gather(dense_mine, 'fsdp', axis=0, tiled=True)  68.1 us
    all_gather x1, waiting for transfers between devices, on_device(): lax.all_gather(expert_in.reshape(units, EXPERTS * model_width), 'fsdp', a...  65.3 us
    unnamed x253, local copies, waits for them, and re-layouts  43 us
  transfers between devices with their start and end apart: 10, of which 6 were waited for; matrix products, arithmetic and copies ran while one was open for 20% of the time, Pallas kernels for 0%

commit v1 on v0

--- a/solution.py
+++ b/solution.py
@@ -89,7 +89,14 @@
     dense_mine = jnp.concatenate(
         [jnp.concatenate([qkv_weight, proj_weight], axis=1), small_mine], axis=0
     )
-    dense = lax.all_gather(dense_mine, "fsdp", axis=0, tiled=True)
+    ways, here_2 = (lax.axis_size("fsdp"), lax.axis_index("fsdp"))
+    dense, reach = (dense_mine, 1)
+    while reach < ways:
+        other = lax.ppermute(dense, "fsdp", [(d, d ^ reach) for d in range(ways)])
+        mine_first = jnp.concatenate([dense, other], axis=0)
+        theirs_first = jnp.concatenate([other, dense], axis=0)
+        dense = jnp.where(here_2 & reach == 0, mine_first, theirs_first)
+        reach = 2 * reach
     dense = dense.reshape(n_dev, own + SMALL_ROWS, wide)
     w_in = lax.all_gather(
         expert_in.reshape(units, EXPERTS * model_width),

time: 884 us -> 949 us (1.074)
  waiting for transfers between devices: 595 us -> 652 us
  local copies, waits for them, and re-layouts: 114 us -> 104 us
  other arithmetic: 36 us -> 45.5 us
    ppermute x0 -> x5, waiting for transfers between devices: none -> 277 us  [on_device(): other = lax.ppermute(dense, 'fsdp', [(d, d ^ reach) for d in range(ways)])]
    all_gather x1, waiting for transfers between devices: 114 us -> 27.5 us  [on_device(): lax.all_gather(expert_out.reshape(units, EXPERTS * model_width), 'fsdp',...]
    all_gather x1 -> x0, waiting for transfers between devices: 68.1 us -> none  [on_device(): dense = lax.all_gather(dense_mine, 'fsdp', axis=0, tiled=True)]
    all_gather x1, waiting for transfers between devices: 65.3 us -> 0.01 us  [on_device(): lax.all_gather(expert_in.reshape(units, EXPERTS * model_width), 'fsdp', a...]
    select_n x0 -> x5, other arithmetic: none -> 9.73 us  [on_device(): dense = jnp.where(here_2 & reach == 0, mine_first, theirs_first)]
    unnamed x8 -> x7, waiting for transfers between devices: 240 us -> 239 us
    unnamed x253 -> x288, local copies, waits for them, and re-layouts: 43 us -> 42.9 us
  transfers between devices with their start and end apart: 10 -> 14, of which waited for: 6 -> 9; matrix products, arithmetic and copies ran while one was open for 20% -> 19% of each run, Pallas kernels for 0% -> 0%
where the time goes in v1:
time: 949 us; the launch traced here: 939 us
  waiting for transfers between devices  652 us (69%)
  matrix products  114 us (12%)
  local copies, waits for them, and re-layouts  104 us (11%)
  other arithmetic  45.5 us (5%)
  between operations  16.4 us (2%)
    ppermute x5, waiting for transfers between devices, on_device(): other = lax.ppermute(dense, 'fsdp', [(d, d ^ reach) for d in range(ways)])  277 us
    unnamed x7, waiting for transfers between devices  239 us
    reduce_scatter x1, waiting for transfers between devices, on_device(): lax.psum_scatter(dense_grads.reshape(n_dev * (own + SMALL_ROWS), wide), '...  108 us
    dot_general x33, matrix products, dot_f32(): lax.dot_general(left, right, (((left_dim,), (right_dim,)), ((), ())), pre...  87.3 us
    unnamed x288, local copies, waits for them, and re-layouts  42.9 us
    all_gather x1, waiting for transfers between devices, on_device(): lax.all_gather(expert_out.reshape(units, EXPERTS * model_width), 'fsdp',...  27.5 us
  transfers between devices with their start and end apart: 14, of which 9 were waited for; matrix products, arithmetic and copies ran while one was open for 19% of the time, Pallas kernels for 0%

profile of v1, /device:TPU:0, one launch (start us, length us, event | category | flops | bytes accessed | tf_op | source)
XLA Modules:
  0.0 939.5 jit_solution(14971593964026752716)
XLA Ops:
  13.7 2.9 collective-permute-start.1
  16.6 11.3 %collective-permute-done.1 = bf16[64,3072]{1,0:T(8,128)(2,1)S(1)} collective-permute-done((bf16[64,3072]{1,0:T(8,128)(2,1)S(1)}, bf16[64,3072]{1,0:T(8,128)(2,1)S(1)}, u32[]{:S(2)}, u32[]{:S(2)}) %collective-permute-start.1) | collective-permute-done | bytes 393248 | tf_op jit(solution)/shard_map/ppermute | solution.py:95
  29.5 17.3 %collective-permute-done.2 = bf16[128,3072]{1,0:T(8,128)(2,1)S(1)} collective-permute-done((bf16[128,3072]{1,0:T(8,128)(2,1)S(1)}, bf16[128,3072]{1,0:T(8,128)(2,1)S(1)}, u32[]{:S(2)}, u32[]{:S(2)}) %collective-permute-start.2) | collective-permute-done | bytes 786464 | tf_op jit(solution)/shard_map/ppermute | solution.py:95
  48.8 64.5 %collective-permute-done.3 = bf16[256,3072]{1,0:T(8,128)(2,1)} collective-permute-done((bf16[256,3072]{1,0:T(8,128)(2,1)S(1)}, bf16[256,3072]{1,0:T(8,128)(2,1)}, u32[]{:S(2)}, u32[]{:S(2)}) %collective-permute-start.3) | collective-permute-done | bytes 1572896 | tf_op jit(solution)/shard_map/ppermute | solution.py:95
  113.2 3.5 maximum_select_fusion.1
  120.1 183.3 %collective-permute-done.4 = bf16[512,3072]{1,0:T(8,128)(2,1)} collective-permute-done((bf16[512,3072]{1,0:T(8,128)(2,1)S(1)}, bf16[512,3072]{1,0:T(8,128)(2,1)}, u32[]{:S(2)}, u32[]{:S(2)}) %collective-permute-start.4) | collective-permute-done | bytes 3145760 | tf_op jit(solution)/shard_map/ppermute | solution.py:95
  303.5 5.6 maximum_select_fusion
  309.3 2.5 slice.421
  314.4 3.8 fusion.33
  329.2 2.4 copy.104
  331.6 3.8 fusion.177
  335.4 3.0 fusion.90
  344.4 2.6 bitcast_reduce_fusion
  347.0 2.5 convolution_convert_fusion.10
  351.3 2.4 fusion.175
  353.7 2.4 fusion.174
  356.1 2.5 slice_bitcast_fusion.14
  358.6 2.5 slice_bitcast_fusion.15
  361.2 5.7 multiply_convert_fusion.4
  368.1 2.9 convolution_convert_fusion.8
  371.0 27.5 %all-gather.5.cloned.1.call-done = bf16[1536,3072]{1,0:T(8,128)(2,1)} async-done(((bf16[96,3072]{1,0:T(8,128)(2,1)}), bf16[1536,3072]{1,0:T(8,128)(2,1)}) %all-gather.5.cloned.1.call-update) | async-done | bytes 9437200 | tf_op jit(solution)/shard_map/all_gather | solution.py:108
  398.5 6.2 fusion.9
  406.5 3.8 multiply_convert_fusion.1
  411.7 4.9 fusion.30
  422.2 4.6 fusion.23
  431.9 4.6 fusion.16
  438.7 4.4 pad_maximum_fusion
  443.1 4.4 pad_maximum_fusion.1
  447.5 12.6 %copy.130 = bf16[1536,3072]{1,0:T(8,128)(2,1)} copy(bf16[1536,3072]{0,1:T(8,128)(2,1)} %pad_maximum_fusion) | data formatting | bytes 18874368
  460.2 12.7 %copy.132 = bf16[1536,3072]{1,0:T(8,128)(2,1)} copy(bf16[1536,3072]{0,1:T(8,128)(2,1)} %pad_maximum_fusion.1) | data formatting | bytes 18874368
  474.1 3.7 fusion.53
  477.8 4.2 fusion.47
  489.3 2.6 fusion.68
  491.9 2.5 fusion.62
  494.4 2.6 fusion.59
  499.2 3.6 fusion.65
  507.0 2.9 fusion.125
  512.1 2.7 fusion.117
  525.4 3.4 fusion.180
  531.6 3.5 multiply_reduce_fusion
  535.1 3.3 multiply_convert_fusion
  541.0 3.4 reshape.444
  550.3 5.2 fusion.169
  562.0 3.5 fusion.2
  565.4 64.2 %reduce-scatter.10.cloned.1.call-done = bf16[96,3072]{1,0:T(8,128)(2,1)} async-done(((bf16[1536,3072]{1,0:T(8,128)(2,1)}), bf16[96,3072]{1,0:T(8,128)(2,1)}) %reduce-scatter.10.cloned.1.call-update) | async-done | bytes 589840
  631.9 174.4 %reduce-scatter.12.cloned.1.call-done = bf16[96,3072]{1,0:T(8,128)(2,1)} async-done(((bf16[1536,3072]{1,0:T(8,128)(2,1)}), bf16[96,3072]{1,0:T(8,128)(2,1)}) %reduce-scatter.12.cloned.1.call-update) | async-done | bytes 589840
  809.8 2.8 add_add_fusion.2
  817.1 108.2 %reduce-scatter.8.cloned.1.call-done = bf16[32,3072]{1,0:T(8,128)(2,1)} async-done(((bf16[1024,3072]{1,0:T(8,128)(2,1)}), bf16[32,3072]{1,0:T(8,128)(2,1)}) %reduce-scatter.8.cloned.1.call-update) | async-done | bytes 196624 | tf_op jit(solution)/shard_map/reduce_scatter | solution.py:297
  (458 shorter events, 113.4 us)
Async XLA Ops:
  7.3 353.9 %all-gather.3.cloned.1.call-start = ((), (), s32[]{:S(2)}) async-start(), calls=%async_computation.3 | async-start | bytes 10027008 | tf_op jit(solution)/shard_map/all_gather | solution.py:101
  9.4 389.1 %all-gather.5.cloned.1.call-start = ((), (), s32[]{:S(2)}) async-start(), calls=%async_computation.4 | async-start | bytes 10027008 | tf_op jit(solution)/shard_map/all_gather | solution.py:108
  11.4 618.2 %reduce-scatter.10.cloned.1.call-start = ((), (), s32[]{:S(2)}) async-start(), calls=%async_computation.6 | async-start | bytes 10027008
  12.0 1.6 collective-permute-start
  13.7 14.2 %collective-permute-start.1 = (bf16[64,3072]{1,0:T(8,128)(2,1)S(1)}, bf16[64,3072]{1,0:T(8,128)(2,1)S(1)}, u32[]{:S(2)}, u32[]{:S(2)}) collective-permute-start(bf16[64,3072]{1,0:T(8,128)(2,1)S(1)} %maximum_select_fusion.4), channel_id=1, source_target_pairs={{0,2},{1,3},{2,0},{3,1},{4,6},{5,7},{6,4},{7,5},{8,10},{9,11},{10,... | collective-permute-start | bytes 1179656 | tf_op jit(solution)/shard_map/ppermute | solution.py:95
  28.1 18.8 %collective-permute-start.2 = (bf16[128,3072]{1,0:T(8,128)(2,1)S(1)}, bf16[128,3072]{1,0:T(8,128)(2,1)S(1)}, u32[]{:S(2)}, u32[]{:S(2)}) collective-permute-start(bf16[128,3072]{1,0:T(8,128)(2,1)S(1)} %maximum_select_fusion.3), channel_id=1, source_target_pairs={{0,4},{1,5},{2,6},{3,7},{4,0},{5,1},{6,2},{7,3},{8,12},{9,13},{10,... | collective-permute-start | bytes 2359304 | tf_op jit(solution)/shard_map/ppermute | solution.py:95
  47.2 66.0 %collective-permute-start.3 = (bf16[256,3072]{1,0:T(8,128)(2,1)S(1)}, bf16[256,3072]{1,0:T(8,128)(2,1)}, u32[]{:S(2)}, u32[]{:S(2)}) collective-permute-start(bf16[256,3072]{1,0:T(8,128)(2,1)S(1)} %maximum_select_fusion.2), channel_id=1, source_target_pairs={{0,8},{1,9},{2,10},{3,11},{4,12},{5,13},{6,14},{7,15},{8,0},{9,1},... | collective-permute-start | bytes 4718600 | tf_op jit(solution)/shard_map/ppermute | solution.py:95
  48.8 70.7 %copy-start.98 = (s32[394,2]{0,1:T(2,128)S(1)}, s32[394,2]{0,1:T(2,128)}, u32[]{:S(2)}) copy-start(s32[394,2]{0,1:T(2,128)} %param.30) | copy-start | bytes 9460
  116.7 186.7 %collective-permute-start.4 = (bf16[512,3072]{1,0:T(8,128)(2,1)S(1)}, bf16[512,3072]{1,0:T(8,128)(2,1)}, u32[]{:S(2)}, u32[]{:S(2)}) collective-permute-start(bf16[512,3072]{1,0:T(8,128)(2,1)S(1)} %maximum_select_fusion.1), channel_id=1, source_target_pairs={{0,16},{1,17},{2,18},{3,19},{4,20},{5,21},{6,22},{7,23},{8,24},{9,... | collective-permute-start | bytes 9437192 | tf_op jit(solution)/shard_map/ppermute | solution.py:95
  118.1 196.3 %copy-start.80 = (f32[394]{0:T(512)}, f32[394]{0:T(512)S(1)}, u32[]{:S(2)}) copy-start(f32[394]{0:T(512)S(1)} %broadcast_multiply_fusion.1) | copy-start | bytes 4732
  119.5 194.9 %copy-start.96 = (f32[394]{0:T(512)}, f32[394]{0:T(512)S(1)}, u32[]{:S(2)}) copy-start(f32[394]{0:T(512)S(1)} %fusion.142) | copy-start | bytes 4732
  309.3 5.1 copy-start.4
  313.4 30.0 %copy-start.82 = (bf16[1,768]{1,0:T(2,128)(2,1)}, bf16[1,768]{1,0:T(2,128)(2,1)S(1)}, u32[]{:S(2)}) copy-start(bf16[1,768]{1,0:T(2,128)(2,1)S(1)} %stack_reshape.15) | copy-start | bytes 4612
  313.5 29.9 %copy-start.84 = (bf16[1,768]{1,0:T(2,128)(2,1)}, bf16[1,768]{1,0:T(2,128)(2,1)S(1)}, u32[]{:S(2)}) copy-start(bf16[1,768]{1,0:T(2,128)(2,1)S(1)} %stack_reshape.14) | copy-start | bytes 4612
  313.6 29.8 %copy-start.86 = (bf16[1,768]{1,0:T(2,128)(2,1)}, bf16[1,768]{1,0:T(2,128)(2,1)S(1)}, u32[]{:S(2)}) copy-start(bf16[1,768]{1,0:T(2,128)(2,1)S(1)} %stack_reshape.13) | copy-start | bytes 4612
  313.7 29.7 %copy-start.88 = (bf16[1,768]{1,0:T(2,128)(2,1)}, bf16[1,768]{1,0:T(2,128)(2,1)S(1)}, u32[]{:S(2)}) copy-start(bf16[1,768]{1,0:T(2,128)(2,1)S(1)} %stack_reshape.12) | copy-start | bytes 4612
  313.9 29.2 %copy-start.66 = (f32[768]{0:T(1024)}, f32[768]{0:T(1024)S(1)}, u32[]{:S(2)}) copy-start(f32[768]{0:T(1024)S(1)} %reshape.458) | copy-start | bytes 9220
  322.8 8.8 copy-start.8
  327.1 8.3 copy-start.6
  342.8 175.8 %copy-start = (f32[394,768]{1,0:T(8,128)}, f32[394,768]{1,0:T(8,128)S(1)}, u32[]{:S(2)}) copy-start(f32[394,768]{1,0:T(8,128)S(1)} %get-tuple-element.184) | copy-start | bytes 3631108
  344.1 167.5 %copy-start.63 = (f32[394,4]{0,1:T(4,128)}, f32[394,4]{0,1:T(4,128)S(1)}, u32[]{:S(2)}) copy-start(f32[394,4]{0,1:T(4,128)S(1)} %get-tuple-element.124) | copy-start | bytes 18916
  344.1 170.7 %copy-start.101 = (s32[394,1]{0,1:T(1,128)}, s32[394,1]{0,1:T(1,128)S(1)}, u32[]{:S(2)}) copy-start(s32[394,1]{0,1:T(1,128)S(1)} %get-tuple-element.177) | copy-start | bytes 4732
  344.1 170.7 %copy-start.103 = (s32[394,1]{0,1:T(1,128)}, s32[394,1]{0,1:T(1,128)S(1)}, u32[]{:S(2)}) copy-start(s32[394,1]{0,1:T(1,128)S(1)} %get-tuple-element.178) | copy-start | bytes 4732
  347.0 9.1 collective-permute-start.6
  349.5 9.1 collective-permute-start.5
  361.2 6.9 copy-start.56
  361.2 6.9 copy-start.58
  398.5 6.2 copy-start.54
  398.5 6.3 copy-start.59
  410.3 7.9 slice-start
  411.7 6.5 slice-start.1
  411.7 6.5 slice-start.2
  460.2 346.1 %reduce-scatter.12.cloned.1.call-start = ((), (), s32[]{:S(2)}) async-start(), calls=%async_computation.7 | async-start | bytes 10027008
  472.9 452.4 %reduce-scatter.8.cloned.1.call-start = ((), (), s32[]{:S(2)}) async-start(), calls=%async_computation.5 | async-start | bytes 6488064 | tf_op jit(solution)/shard_map/reduce_scatter | solution.py:297
  474.1 8.1 slice-start.6
  474.1 8.1 slice-start.7
  482.2 6.2 slice-start.4
  487.1 19.9 %collective-permute-start.7 = (bf16[4,256,768]{2,1,0:T(8,128)(2,1)}, bf16[4,256,768]{2,1,0:T(8,128)(2,1)}, u32[]{:S(2)}, u32[]{:S(2)}) collective-permute-start(bf16[4,256,768]{2,1,0:T(8,128)(2,1)} %pad_maximum_fusion.3), channel_id=1, source_target_pairs={{0,1},{1,0},{2,3},{3,2},{4,5},{5,4},{6,7},{7,6},{8,9},{9,8},{10,11... | collective-permute-start | bytes 4718600 | tf_op jit(solution)/shard_map/ppermute | solution.py:172
  506.1 6.0 collective-permute-start.8
  539.3 5.1 copy-start.7
  550.2 5.3 copy-start.60
  550.2 5.3 copy-start.93
  550.2 5.3 copy-start.97
  550.2 6.2 copy-start.79
  550.2 6.2 copy-start.78
  550.3 6.2 copy-start.77
  550.3 6.2 copy-start.76
  550.3 6.3 copy-start.75
  (100 other events, 245.1 us)
Sparse Core Ops, SparseCore 0:
  11.5 230.4 all-gather.2
  245.4 153.0 all-gather.4
  460.3 169.2 reduce-scatter.9
  636.1 170.1 reduce-scatter.11
  811.7 113.5 reduce-scatter.7
